TPU v7x, 32 devices: a whole 2x2x4 slice. The times are simulated.
32 devices in a mesh: seq: 4 (over x, core), ctx: 8 (over z, y).
Axes of the slice: x: 2, y: 2, z: 4, core: 2. Of those that a mesh axis runs over, the one named last changes fastest.
Arguments:
- grad_out: bfloat16 [4, 1024, 4096], P('seq', 'ctx'), may hold values from -6 to 6
- inputs: bfloat16 [4, 1024, 4096], P('seq', 'ctx'), may hold values from -6 to 6
- residues: float32 [16, 256], replicated, may hold values from -4 to 4
- rates: float32 [16, 256], replicated, may hold values from 9.765625e-05 to 0.0625
Outputs:
- grad_in: float32 [4, 1024, 4096], P('seq', 'ctx')
- grad_residues: float32 [16, 256], replicated
All inputs are finite; a program needn't handle non-finite values.
Results may differ from a plain program's by a relative error of at most 0.0003.
Values sent between devices are 32-bit elements; how exact they have to be, the bound alone decides.
A program may use at most 128 MiB of HBM per device.

v0:
```python
import jax
import jax.numpy as jnp
from jax import lax
from jax.sharding import PartitionSpec as P


def prefix(part, axis, combine, identity):
    count = lax.axis_size(axis)
    place = lax.axis_index(axis)
    ahead = count - 1 - place
    gathered = jax.tree.map(lambda a: lax.all_gather(a, axis), part)
    state = jax.tree.map(lambda a, e: jnp.zeros_like(a) + jnp.asarray(e, a.dtype), part, identity)

    def one(turn, state):
        source = count - 1 - turn
        return combine(
            state, jax.tree.map(lambda a: lax.dynamic_index_in_dim(a, source, 0, False), gathered)
        )

    return lax.fori_loop(0, ahead, one, state)


def local(grad_out, inputs, residues, rates):
    own_rows = grad_out.shape[1]
    model_width = grad_out.shape[2]
    mode_count = residues.shape[0]
    groups = residues.shape[1]
    per_group = model_width // groups
    shards = lax.axis_size("ctx")
    seq_count = lax.axis_size("seq")
    group_block = min(groups, 16)
    block_count = groups // group_block
    highest = lax.Precision.HIGHEST
    positions = jnp.arange(own_rows, dtype=jnp.float32)
    decays = jnp.exp(-rates[:, :, None] * positions)
    remaining = jnp.exp(-rates[:, :, None] * (own_rows - positions))
    amplitude = residues * jnp.sqrt(-jnp.expm1(-2.0 * rates) / mode_count)
    kernel = jnp.sum(amplitude[:, :, None] * decays, axis=0)
    lag_index = lax.broadcasted_iota(jnp.int32, (own_rows, own_rows), 1) - lax.broadcasted_iota(
        jnp.int32, (own_rows, own_rows), 0
    )
    causal = lag_index >= 0
    clipped = jnp.clip(lag_index, 0, own_rows - 1)
    row_of = lax.broadcasted_iota(jnp.int32, (own_rows, own_rows), 0)
    col_of = lax.broadcasted_iota(jnp.int32, (own_rows, own_rows), 1)
    diagonal_mask = row_of + col_of < own_rows
    grad_rows = grad_out[0].reshape(own_rows, groups, per_group)
    in_rows = inputs[0].reshape(own_rows, groups, per_group)

    def one_block(position):
        first_group = position * group_block
        grad_piece = lax.dynamic_slice_in_dim(grad_rows, first_group, group_block, 1)
        input_piece = lax.dynamic_slice_in_dim(in_rows, first_group, group_block, 1)
        kernel_piece = lax.dynamic_slice_in_dim(kernel, first_group, group_block, 0)
        decay_piece = lax.dynamic_slice_in_dim(decays, first_group, group_block, 1)
        tail_piece = lax.dynamic_slice_in_dim(remaining, first_group, group_block, 1)
        toeplitz = jnp.where(causal[None], jnp.take(kernel_piece, clipped, axis=1), 0.0)
        grad_wide = grad_piece.astype(jnp.float32)
        local_in = jnp.einsum("gst,tgc->sgc", toeplitz, grad_wide, precision=highest)
        summary = jnp.einsum("ngt,tgc->ngc", decay_piece, grad_wide, precision=highest)
        tail_weight = jnp.einsum(
            "ngs,sgc->ngc", tail_piece, input_piece.astype(jnp.float32), precision=highest
        )
        products = jnp.einsum(
            "sgc,tgc->gst", input_piece, grad_piece, preferred_element_type=jnp.float32
        )
        flattened = products.reshape(group_block, own_rows * own_rows)
        flattened = jnp.pad(flattened, ((0, 0), (0, own_rows)))
        skewed = flattened.reshape(group_block, own_rows, own_rows + 1)[:, :, :own_rows]
        lagged = jnp.sum(jnp.where(diagonal_mask[None], skewed, 0.0), axis=1)
        local_grad = jnp.sum(decay_piece * lagged[None], axis=2)
        return (local_in, summary, tail_weight, local_grad)

    local_in, summary, tail_weight, local_grad = lax.map(
        one_block, jnp.arange(block_count, dtype=jnp.int32)
    )
    local_in = jnp.moveaxis(local_in, 0, 1).reshape(own_rows, groups, per_group)
    summary = jnp.moveaxis(summary, 0, 1).reshape(mode_count, model_width)
    tail_weight = jnp.moveaxis(tail_weight, 0, 1).reshape(mode_count, groups, per_group)
    local_grad = jnp.moveaxis(local_grad, 0, 1).reshape(mode_count, groups)
    decay_shard = jnp.exp(-rates * own_rows)

    def compose(earlier, latter):
        joined = latter[0].reshape(mode_count, groups, per_group) + latter[1][:, :, None] * earlier[
            0
        ].reshape(mode_count, groups, per_group)
        return (joined.reshape(mode_count, model_width), latter[1] * earlier[1])

    identity = (
        jnp.zeros((mode_count, model_width), jnp.float32),
        jnp.ones((mode_count, groups), jnp.float32),
    )
    scanned = prefix((summary, decay_shard), "ctx", compose, identity)
    incoming = scanned[0].reshape(mode_count, groups, per_group)
    carry_in = jnp.einsum(
        "ngs,ngc->sgc", amplitude[:, :, None] * remaining, incoming, precision=highest
    )
    grad_in = (local_in + carry_in).reshape(1, own_rows, model_width)
    partial_value = local_grad + jnp.sum(tail_weight * incoming, axis=2)
    total = lax.psum(partial_value, ("seq", "ctx"))
    factor = jnp.sqrt(-jnp.expm1(-2.0 * rates) / float(seq_count * shards * own_rows * per_group))
    return (grad_in, total * factor)


def solution(mesh):
    placed = (P("seq", "ctx", None), P("seq", "ctx", None), P(), P())
    return jax.shard_map(
        local, mesh=mesh, in_specs=placed, out_specs=(P("seq", "ctx", None), P()), check_vma=False
    )
```

profile of v0, /device:TPU:0, one launch (start us, length us, event | category | flops | bytes accessed | tf_op | source)
XLA Modules:
  0.0 1325.7 jit_solution(14390200035358126921)
XLA Ops:
  15.8 1175.9 %while.35 = (s32[]{:T(128)}, f32[16,128,16,16]{1,3,2,0:T(8,128)}, f32[16,16,16,16]{1,3,2,0:T(8,128)}, f32[16,16,16,16]{1,3,2,0:T(8,128)}, f32[16,16,16]{1,2,0:T(...) while((s32[]{:T(128)}, f32[16,128,16,16]{1,3,2,0:T(8,128)}, ...), condition=%wide.region_4.5_spmd.clone.clone, body=%wide.region_1.4_spmd.clone.clone.sunk | while | flops 72693504 | bytes 15064287 | solution.py:74
  17.3 54.4 %gather_fusion = f32[16384,16]{1,0:T(8,128)} fusion(f32[16,128]{0,1:T(8,128)S(1)} %copy.46, s32[16384]{0:T(1024)S(1)} %fusion.68), kind=kCustom, calls=%fused_computation.clone.clone.1 | custom fusion | bytes 2162688 | tf_op jit(solution)/shard_map/while/body/eval_jaxpr/jit(_take)/gather | solution.py:57
  90.8 54.4 %gather_fusion = f32[16384,16]{1,0:T(8,128)} fusion(f32[16,128]{0,1:T(8,128)S(1)} %copy.46, s32[16384]{0:T(1024)S(1)} %fusion.68), kind=kCustom, calls=%fused_computation.clone.clone.1 | custom fusion | bytes 2162688 | tf_op jit(solution)/shard_map/while/body/eval_jaxpr/jit(_take)/gather | solution.py:57
  145.2 5.2 copy.47
  164.3 54.4 %gather_fusion = f32[16384,16]{1,0:T(8,128)} fusion(f32[16,128]{0,1:T(8,128)S(1)} %copy.46, s32[16384]{0:T(1024)S(1)} %fusion.68), kind=kCustom, calls=%fused_computation.clone.clone.1 | custom fusion | bytes 2162688 | tf_op jit(solution)/shard_map/while/body/eval_jaxpr/jit(_take)/gather | solution.py:57
  237.8 54.4 %gather_fusion = f32[16384,16]{1,0:T(8,128)} fusion(f32[16,128]{0,1:T(8,128)S(1)} %copy.46, s32[16384]{0:T(1024)S(1)} %fusion.68), kind=kCustom, calls=%fused_computation.clone.clone.1 | custom fusion | bytes 2162688 | tf_op jit(solution)/shard_map/while/body/eval_jaxpr/jit(_take)/gather | solution.py:57
  292.2 5.2 copy.47
  311.3 54.4 %gather_fusion = f32[16384,16]{1,0:T(8,128)} fusion(f32[16,128]{0,1:T(8,128)S(1)} %copy.46, s32[16384]{0:T(1024)S(1)} %fusion.68), kind=kCustom, calls=%fused_computation.clone.clone.1 | custom fusion | bytes 2162688 | tf_op jit(solution)/shard_map/while/body/eval_jaxpr/jit(_take)/gather | solution.py:57
  384.8 54.4 %gather_fusion = f32[16384,16]{1,0:T(8,128)} fusion(f32[16,128]{0,1:T(8,128)S(1)} %copy.46, s32[16384]{0:T(1024)S(1)} %fusion.68), kind=kCustom, calls=%fused_computation.clone.clone.1 | custom fusion | bytes 2162688 | tf_op jit(solution)/shard_map/while/body/eval_jaxpr/jit(_take)/gather | solution.py:57
  458.3 54.4 %gather_fusion = f32[16384,16]{1,0:T(8,128)} fusion(f32[16,128]{0,1:T(8,128)S(1)} %copy.46, s32[16384]{0:T(1024)S(1)} %fusion.68), kind=kCustom, calls=%fused_computation.clone.clone.1 | custom fusion | bytes 2162688 | tf_op jit(solution)/shard_map/while/body/eval_jaxpr/jit(_take)/gather | solution.py:57
  531.8 54.4 %gather_fusion = f32[16384,16]{1,0:T(8,128)} fusion(f32[16,128]{0,1:T(8,128)S(1)} %copy.46, s32[16384]{0:T(1024)S(1)} %fusion.68), kind=kCustom, calls=%fused_computation.clone.clone.1 | custom fusion | bytes 2162688 | tf_op jit(solution)/shard_map/while/body/eval_jaxpr/jit(_take)/gather | solution.py:57
  605.3 54.4 %gather_fusion = f32[16384,16]{1,0:T(8,128)} fusion(f32[16,128]{0,1:T(8,128)S(1)} %copy.46, s32[16384]{0:T(1024)S(1)} %fusion.68), kind=kCustom, calls=%fused_computation.clone.clone.1 | custom fusion | bytes 2162688 | tf_op jit(solution)/shard_map/while/body/eval_jaxpr/jit(_take)/gather | solution.py:57
  678.8 54.4 %gather_fusion = f32[16384,16]{1,0:T(8,128)} fusion(f32[16,128]{0,1:T(8,128)S(1)} %copy.46, s32[16384]{0:T(1024)S(1)} %fusion.68), kind=kCustom, calls=%fused_computation.clone.clone.1 | custom fusion | bytes 2162688 | tf_op jit(solution)/shard_map/while/body/eval_jaxpr/jit(_take)/gather | solution.py:57
  752.3 54.4 %gather_fusion = f32[16384,16]{1,0:T(8,128)} fusion(f32[16,128]{0,1:T(8,128)S(1)} %copy.46, s32[16384]{0:T(1024)S(1)} %fusion.68), kind=kCustom, calls=%fused_computation.clone.clone.1 | custom fusion | bytes 2162688 | tf_op jit(solution)/shard_map/while/body/eval_jaxpr/jit(_take)/gather | solution.py:57
  825.8 54.4 %gather_fusion = f32[16384,16]{1,0:T(8,128)} fusion(f32[16,128]{0,1:T(8,128)S(1)} %copy.46, s32[16384]{0:T(1024)S(1)} %fusion.68), kind=kCustom, calls=%fused_computation.clone.clone.1 | custom fusion | bytes 2162688 | tf_op jit(solution)/shard_map/while/body/eval_jaxpr/jit(_take)/gather | solution.py:57
  899.2 54.4 %gather_fusion = f32[16384,16]{1,0:T(8,128)} fusion(f32[16,128]{0,1:T(8,128)S(1)} %copy.46, s32[16384]{0:T(1024)S(1)} %fusion.68), kind=kCustom, calls=%fused_computation.clone.clone.1 | custom fusion | bytes 2162688 | tf_op jit(solution)/shard_map/while/body/eval_jaxpr/jit(_take)/gather | solution.py:57
  972.7 54.4 %gather_fusion = f32[16384,16]{1,0:T(8,128)} fusion(f32[16,128]{0,1:T(8,128)S(1)} %copy.46, s32[16384]{0:T(1024)S(1)} %fusion.68), kind=kCustom, calls=%fused_computation.clone.clone.1 | custom fusion | bytes 2162688 | tf_op jit(solution)/shard_map/while/body/eval_jaxpr/jit(_take)/gather | solution.py:57
  1046.2 54.4 %gather_fusion = f32[16384,16]{1,0:T(8,128)} fusion(f32[16,128]{0,1:T(8,128)S(1)} %copy.46, s32[16384]{0:T(1024)S(1)} %fusion.68), kind=kCustom, calls=%fused_computation.clone.clone.1 | custom fusion | bytes 2162688 | tf_op jit(solution)/shard_map/while/body/eval_jaxpr/jit(_take)/gather | solution.py:57
  1119.7 54.4 %gather_fusion = f32[16384,16]{1,0:T(8,128)} fusion(f32[16,128]{0,1:T(8,128)S(1)} %copy.46, s32[16384]{0:T(1024)S(1)} %fusion.68), kind=kCustom, calls=%fused_computation.clone.clone.1 | custom fusion | bytes 2162688 | tf_op jit(solution)/shard_map/while/body/eval_jaxpr/jit(_take)/gather | solution.py:57
  1194.6 32.5 %all-gather = f32[128,256]{1,0:T(8,128)S(1)} all-gather(f32[16,256]{1,0:T(8,128)S(1)} %copy-done.3), channel_id=2, replica_groups=mesh['seq'=4,'ctx'=8] {'ctx'}, dimensions={0}, use_global_device_ids=true | all-gather | bytes 147456 | tf_op jit(solution)/shard_map/all_gather | solution.py:11
  1227.2 19.8 %all-gather.3.cloned.1.call-done = f32[8,16,4096]{2,1,0:T(8,128)} async-done(((f32[1,16,4096]{2,1,0:T(8,128)}), f32[8,16,4096]{2,1,0:T(8,128)}) %all-gather.3.cloned.1.call-update) | async-done | bytes 2097168 | tf_op jit(solution)/shard_map/all_gather | solution.py:11
  1247.0 23.0 %while.34 = (s32[]{:T(128)}, f32[16,4096]{1,0:T(8,128)S(1)}, s32[]{:T(128)}, f32[8,16,4096]{2,1,0:T(8,128)}, f32[8,16,256]{2,1,0:T(8,128)S(1)}, /*index=5*/s32[]{:T(128)}, s32[]{:T(128)}, s32[]{:T(128)}, s32[]{:T(128)}) while((s32[]{:T(128)}, f32[16,4096]{1,0:T(8,128)S(1)}, s32[]{:T(128)}, f32[8,16,4096]{2,1,0:T(8,128)}, ...), condition=%wide.region_6.7_spmd, body=%wide.region_5.6_spmd.sunk | while | flops 131078 | bytes 1884307 | solution.py:20
  1272.9 37.0 %psum.7 = f32[16,256]{1,0:T(8,128)S(1)} all-reduce(f32[16,256]{1,0:T(8,128)S(1)} %copy.35), channel_id=1, replica_groups=mesh['seq'=4,'ctx'=8] {'seq','ctx'}, use_global_device_ids=true, to_apply=%region_8.9 | all-reduce | flops 4096 | bytes 32768 | tf_op jit(solution)/shard_map/psum | solution.py:100
  1310.5 5.4 bitcast_add_fusion.1
  (328 shorter events, 322.9 us)
Async XLA Ops:
  7.2 4.0 copy-start
  7.2 1239.8 %all-gather.3.cloned.1.call-start = ((), (), s32[]{:S(2)}) async-start(), calls=%async_computation | async-start | bytes 2359296 | tf_op jit(solution)/shard_map/all_gather | solution.py:11
  1191.7 2.9 copy-start.3
  1270.6 2.3 copy-start.1
  1270.6 39.3 %copy-start.2 = (f32[16,256]{1,0:T(8,128)S(1)}, f32[16,256]{1,0:T(8,128)}, u32[]{:S(2)}) copy-start(f32[16,256]{1,0:T(8,128)} %param.11) | copy-start | bytes 49156
Sparse Core Ops, SparseCore 0:
  1194.7 52.1 all-gather.2
where the time goes:
time: 1330 us
  local copies, waits for them, and re-layouts  1050 us (79%)
  matrix products  123 us (9%)
  blocking collectives  69.5 us (5%)
  other arithmetic  34.5 us (3%)
  waiting for transfers between devices  19.8 us (1%)
  between operations  14.1 us (1%)
    gather x32, local copies, waits for them, and re-layouts, one_block(): jnp.take(kernel_piece, clipped, axis=1)  954 us
    reshape x16, local copies, waits for them, and re-layouts, one_block(): flattened.reshape(group_block, own_rows, own_rows + 1)[:, :, :own_rows]  39.7 us
    dot_general x16, matrix products, one_block(): jnp.einsum('gst,tgc->sgc', toeplitz, grad_wide, precision=highest)  39.4 us
    psum x1, blocking collectives, local(): total = lax.psum(partial_value, ('seq', 'ctx'))  37 us
    all_gather x1, blocking collectives, prefix(): gathered = jax.tree.map(lambda a: lax.all_gather(a, axis), part)  32.5 us
    dot_general x16, matrix products, one_block(): jnp.einsum('ngt,tgc->ngc', decay_piece, grad_wide, precision=highest)  29.2 us
    dot_general x16, matrix products, one_block(): jnp.einsum('ngs,sgc->ngc', tail_piece, input_piece.astype(jnp.float32), p...  29.2 us
  transfers between devices with their start and end apart: 1, of which 1 were waited for; matrix products, arithmetic and copies ran while one was open for 0% of the time, Pallas kernels for 0%

commit v1 on v0

v1 whole, which is shorter than its diff:
```python
import functools

import jax
import jax.numpy as jnp
from jax import lax
from jax.experimental import pallas as pl
from jax.experimental.pallas import tpu as pltpu
from jax.sharding import PartitionSpec as P

MESH = pl.DeviceIdType.MESH
F32 = jnp.float32
BF16 = jnp.bfloat16


def dot(a, b):
    return jnp.dot(a, b, preferred_element_type=F32)


def split(a):
    high = a.astype(BF16)
    return high, (a - high.astype(F32)).astype(BF16)


def one_minus_exp(u):
    series = 1.0 - u * (1.0 / 8.0)
    for order in (7.0, 6.0, 5.0, 4.0, 3.0, 2.0):
        series = 1.0 - u * (1.0 / order) * series
    return u * series


def body(
    shards, seqs, chunks, grad_ref, in_ref, res_ref, rate_ref, out_ref, total_ref,
    own, pair, joined, incoming, outgoing, decay_pow, decay, tail_high, tail_low, tail, lag_sums,
    partial, from_seq, seq_sum, from_ctx,
    pair_send, pair_recv, chain_send, chain_recv, seq_send, seq_recv, ctx_send, ctx_recv,
):
    rows, width = grad_ref.shape
    modes, groups = res_ref.shape
    per_group = width // groups
    tile_groups = modes if modes * per_group == 256 else 256 // per_group
    tile = tile_groups * per_group
    tiles = width // tile
    chunk_tiles = tiles // chunks
    half = 128
    half_groups = half // per_group
    stacked = tile_groups * modes
    pairs = shards // 2

    me = lax.axis_index("ctx")
    my_seq = lax.axis_index("seq")
    upper = me % 2
    place = me // 2
    partner = me + 1 - 2 * upper
    hops = pairs - 1 - place

    barrier = pltpu.get_barrier_semaphore()
    for offset in range(1, shards):
        pl.semaphore_signal(
            barrier, inc=1, device_id={"ctx": lax.rem(me + offset, shards)}, device_id_type=MESH
        )
    for offset in range(1, seqs):
        pl.semaphore_signal(
            barrier, inc=1, device_id={"seq": lax.rem(my_seq + offset, seqs)}, device_id_type=MESH
        )

    lane_group = lax.broadcasted_iota(jnp.int32, (modes, tile), 1) // per_group
    ahead = lax.broadcasted_iota(jnp.int32, (modes, rows), 1).astype(F32)
    behind = float(rows) - ahead

    def rolled(values, index):
        return pltpu.roll(values, lax.rem(groups - index * tile_groups, groups), 1)

    def compress(wide):
        kept = jnp.zeros((modes, tile), F32)
        for g in range(tile_groups):
            kept = jnp.where(lane_group == g, wide[g * modes : (g + 1) * modes, :], kept)
        return kept

    def lanes(index, size):
        return pl.ds(pl.multiple_of(index * size, size), size)

    def pair_copy(q):
        return pltpu.make_async_remote_copy(
            own.at[q], pair.at[q], pair_send.at[q], pair_recv.at[q],
            device_id={"ctx": partner}, device_id_type=MESH,
        )

    def chain_copy(q):
        return pltpu.make_async_remote_copy(
            outgoing.at[q], incoming.at[q], chain_send.at[q], chain_recv.at[q],
            device_id={"ctx": lax.rem(me + shards - 2, shards)}, device_id_type=MESH,
        )

    for q in range(chunks):
        def summarize(step, carry, q=q):
            index = q * chunk_tiles + step
            rates = rolled(rate_ref[...], index)
            spread = jnp.zeros((modes, tile), F32)
            parts = []
            for g in range(tile_groups):
                rate = rates[:, g : g + 1]
                parts.append(jnp.exp(-rate * ahead))
                spread = jnp.where(lane_group == g, rate, spread)
            decays = jnp.concatenate(parts, axis=0)
            decay[lanes(index, stacked), :] = decays
            high, low = split(decays)
            grads = grad_ref[:, lanes(index, tile)]
            wide = dot(jnp.concatenate([high, low], axis=1), jnp.concatenate([grads, grads], axis=0))
            own[q, :, lanes(step, tile)] = compress(wide)
            decay_pow[q, :, lanes(step, tile)] = jnp.exp(-float(rows) * spread)
            return carry

        lax.fori_loop(0, chunk_tiles, summarize, 0)
        if q == 0:
            pl.semaphore_wait(barrier, shards - 1 + seqs - 1)
        pair_copy(q).start()

    def exchange(step):
        @pl.when(step < chunks)
        def _():
            pair_copy(step).wait_recv()
            power = decay_pow[step]
            mine, other = own[step], pair[step]
            near = jnp.where(upper == 0, mine, other)
            far = jnp.where(upper == 0, other, mine)
            joined[step] = near + power * far

            @pl.when(hops == 0)
            def _():
                incoming[step] = jnp.zeros(incoming.shape[1:], F32)
                if pairs > 1:
                    outgoing[step] = joined[step]
                    chain_copy(step).start()

        if pairs > 1:
            q = step - hops

            @pl.when((hops > 0) & (q >= 0) & (q < chunks))
            def _():
                chain_copy(q).wait_recv()

                @pl.when(place > 0)
                def _():
                    power = decay_pow[q]
                    outgoing[q] = joined[q] + power * power * incoming[q]
                    chain_copy(q).start()

    steps = chunks + pairs - 1
    per_step = max(1, tiles // steps)

    half_lane_group = lax.broadcasted_iota(jnp.int32, (rows, half), 1) // per_group
    row_of = lax.broadcasted_iota(jnp.int32, (rows, rows), 0)
    col_of = lax.broadcasted_iota(jnp.int32, (rows, rows), 1)
    causal = col_of >= row_of
    inside = col_of <= row_of
    reverse = jnp.where(row_of + col_of == rows - 1, 1.0, 0.0).astype(BF16)
    group_lane = lax.broadcasted_iota(jnp.int32, (modes, groups), 1)
    amplitude = res_ref[...] * jnp.sqrt(one_minus_exp(2.0 * rate_ref[...]) * (1.0 / modes))
    lag_sums[...] = jnp.zeros_like(lag_sums)

    def convolve(index, carry):
        rates = rolled(rate_ref[...], index)
        amps = rolled(amplitude, index)
        tails = []
        weights = []
        sums = lag_sums[...]
        for part in range(tile // half):
            where_half = lanes(index * (tile // half) + part, half)
            grads = grad_ref[:, where_half]
            ins = dot(reverse, in_ref[:, where_half]).astype(BF16)
            doubled = jnp.concatenate([grads, grads], axis=0)
            result = jnp.zeros((rows, half), F32)
            for g8 in range(half_groups):
                g = part * half_groups + g8
                rate = rates[:, g : g + 1]
                amp = amps[:, g : g + 1]
                decays = decay[pl.ds(pl.multiple_of(index * stacked + g * modes, modes), modes), :]
                filt = jnp.sum(amp * decays, axis=0, keepdims=True)
                shifted = pltpu.roll(
                    jnp.broadcast_to(filt, (rows, rows)), 0, 1, stride=1, stride_axis=0
                )
                high, low = split(jnp.where(causal, shifted, 0.0))
                wide = dot(jnp.concatenate([high, low], axis=1), doubled)
                result = jnp.where(half_lane_group == g8, wide, result)
                masked = jnp.where(half_lane_group == g8, ins, jnp.zeros_like(ins))
                products = lax.dot_general(
                    masked, grads, (((1,), (1,)), ((), ())), preferred_element_type=F32
                )
                skewed = pltpu.roll(products, 1, 1, stride=1, stride_axis=0)
                lagged = jnp.sum(jnp.where(inside, skewed, 0.0), axis=0, keepdims=True)
                value = jnp.sum(decays * lagged, axis=1, keepdims=True)
                sums = jnp.where(group_lane == index * tile_groups + g, value, sums)
                remaining = jnp.exp(-rate * behind)
                tails.append(remaining)
                weights.append(amp * remaining)
            out_ref[:, where_half] = result
        lag_sums[...] = sums
        high, low = split(jnp.concatenate(tails, axis=0))
        ins = in_ref[:, lanes(index, tile)]
        wide = dot(jnp.concatenate([high, low], axis=1), jnp.concatenate([ins, ins], axis=0))
        tail[:, lanes(index, tile)] = compress(wide)
        high, low = split(jnp.concatenate(weights, axis=0).T)
        tail_high[index] = high
        tail_low[index] = low

        @pl.when(lax.rem(index, per_step) == per_step - 1)
        def _():
            exchange(index // per_step)

        return carry

    lax.fori_loop(0, tiles, convolve, 0)
    for step in range(tiles // per_step, steps):
        exchange(step)

    def enter(index, sums):
        q, inner = index // chunk_tiles, lax.rem(index, chunk_tiles)
        entry = incoming[q, :, lanes(inner, tile)]
        power = decay_pow[q, :, lanes(inner, tile)]
        entry = jnp.where(upper == 0, pair[q, :, lanes(inner, tile)] + power * entry, entry)
        incoming[q, :, lanes(inner, tile)] = entry
        value = tail[:, lanes(index, tile)] * entry
        high = value.astype(BF16)
        rest = value - high.astype(F32)
        middle, low = split(rest)
        chan_group = lax.broadcasted_iota(jnp.int32, (tile, groups), 0) // per_group
        member = lax.broadcasted_iota(jnp.int32, (tile, groups), 1) == chan_group + index * tile_groups
        member = jnp.where(member, 1.0, 0.0).astype(BF16)
        found = dot(jnp.concatenate([high, middle, low], axis=0), member)
        return sums + found[:modes] + found[modes : 2 * modes] + found[2 * modes :]

    partial[...] = lax.fori_loop(0, tiles, enter, lag_sums[...])

    def seq_copy(offset):
        return pltpu.make_async_remote_copy(
            partial, from_seq.at[offset - 1], seq_send.at[offset - 1], seq_recv.at[offset - 1],
            device_id={"seq": lax.rem(my_seq + offset, seqs)}, device_id_type=MESH,
        )

    def ctx_copy(offset):
        return pltpu.make_async_remote_copy(
            seq_sum, from_ctx.at[offset - 1], ctx_send.at[offset - 1], ctx_recv.at[offset - 1],
            device_id={"ctx": lax.rem(me + offset, shards)}, device_id_type=MESH,
        )

    for offset in range(1, seqs):
        seq_copy(offset).start()

    def carry_in(index, carry):
        q, inner = index // chunk_tiles, lax.rem(index, chunk_tiles)
        entry = incoming[q, :, lanes(inner, tile)]
        blocks = jnp.concatenate(
            [jnp.where(lane_group == g, entry, 0.0) for g in range(tile_groups)], axis=0
        )
        high, low = split(blocks)
        left = tail_high[index]
        out_ref[:, lanes(index, tile)] += dot(
            jnp.concatenate([left, left, tail_low[index]], axis=1),
            jnp.concatenate([high, low, high], axis=0),
        )
        return carry

    lax.fori_loop(0, tiles // 2, carry_in, 0)
    for offset in range(1, seqs):
        seq_copy(offset).wait_recv()

    def ordered(mine, received, place_here, count):
        added = jnp.zeros((modes, groups), F32)
        for source in range(count):
            value = jnp.where(place_here == source, mine, 0.0)
            for offset in range(1, count):
                value = jnp.where(
                    lax.rem(source + offset, count) == place_here, received[offset - 1], value
                )
            added = added + value
        return added

    seq_sum[...] = ordered(partial[...], from_seq, my_seq, seqs)
    for offset in range(1, shards):
        ctx_copy(offset).start()
    lax.fori_loop(tiles // 2, tiles, carry_in, 0)
    for offset in range(1, shards):
        ctx_copy(offset).wait_recv()

    def gather_sum(source, added):
        offset = lax.rem(me - source + shards, shards)
        slot = jnp.maximum(offset - 1, 0)
        return added + jnp.where(offset == 0, seq_sum[...], from_ctx[slot])

    total = lax.fori_loop(0, shards, gather_sum, jnp.zeros((modes, groups), F32))
    scale = 1.0 / float(seqs * shards * rows * per_group)
    total_ref[...] = total * jnp.sqrt(one_minus_exp(2.0 * rate_ref[...]) * scale)

    for q in range(chunks):
        pair_copy(q).wait_send()
        if pairs > 1:
            @pl.when(place > 0)
            def _(q=q):
                chain_copy(q).wait_send()
    for offset in range(1, seqs):
        seq_copy(offset).wait_send()
    for offset in range(1, shards):
        ctx_copy(offset).wait_send()


def local(shards, seqs, grad_out, inputs, residues, rates):
    rows, width = grad_out.shape[1:]
    modes, groups = residues.shape
    chunks = 4
    tile = 256
    chunk_shape = (chunks, modes, width // chunks)
    small = (modes, groups)
    states = pltpu.VMEM(chunk_shape, F32)
    dma = pltpu.SemaphoreType.DMA
    vmem = pl.BlockSpec(memory_space=pltpu.VMEM)
    grad_in, total = pl.pallas_call(
        functools.partial(body, shards, seqs, chunks),
        out_shape=(
            jax.ShapeDtypeStruct((rows, width), F32),
            jax.ShapeDtypeStruct(small, F32),
        ),
        in_specs=[vmem] * 4,
        out_specs=(vmem, vmem),
        scratch_shapes=[
            states, states, states, states, states, states,
            pltpu.VMEM((groups * modes, rows), F32),
            pltpu.VMEM((width // tile, rows, tile // (width // groups) * modes), BF16),
            pltpu.VMEM((width // tile, rows, tile // (width // groups) * modes), BF16),
            pltpu.VMEM((modes, width), F32),
            pltpu.VMEM(small, F32),
            pltpu.VMEM(small, F32),
            pltpu.VMEM((seqs - 1,) + small, F32),
            pltpu.VMEM(small, F32),
            pltpu.VMEM((shards - 1,) + small, F32),
            dma((chunks,)), dma((chunks,)), dma((chunks,)), dma((chunks,)),
            dma((seqs - 1,)), dma((seqs - 1,)), dma((shards - 1,)), dma((shards - 1,)),
        ],
        compiler_params=pltpu.CompilerParams(
            collective_id=0, has_side_effects=True, vmem_limit_bytes=40 * 1024 * 1024
        ),
    )(grad_out[0], inputs[0], residues, rates)
    return grad_in[None], total


def solution(mesh):
    placed = (P("seq", "ctx", None), P("seq", "ctx", None), P(), P())
    return jax.shard_map(
        functools.partial(local, mesh.shape["ctx"], mesh.shape["seq"]),
        mesh=mesh, in_specs=placed, out_specs=(P("seq", "ctx", None), P()), check_vma=False,
    )
```

time: 1330 us -> 58.8 us (0.04)
  local copies, waits for them, and re-layouts: 1050 us -> 5.8 us
  matrix products: 123 us -> 0 us
  blocking collectives: 69.5 us -> 0 us
  Pallas kernels: 0 us -> 52 us
  other arithmetic: 34.5 us -> 0 us
  waiting for transfers between devices: 19.8 us -> 0 us
  between operations: 14.1 us -> 0.65 us
    gather x32 -> x0, local copies, waits for them, and re-layouts: 954 us -> none  [one_block(): jnp.take(kernel_piece, clipped, axis=1)]
    dot_general x65 -> x0, matrix products: 123 us -> none  [the longest x16 39.4 us: one_block(): jnp.einsum('gst,tgc->sgc', toeplitz, grad_wide, precision=highest)]
    pallas_call x0 -> x1, Pallas kernels: none -> 52 us  [local(): pl.pallas_call(functools.partial(body, shards, seqs, chunks), out_shape=(...]
    reshape x17 -> x0, local copies, waits for them, and re-layouts: 40.3 us -> none  [the longest x16 39.7 us: one_block(): flattened.reshape(group_block, own_rows, own_rows + 1)[:, :, :own_rows]]
    psum x1 -> x0, blocking collectives: 37 us -> none  [local(): total = lax.psum(partial_value, ('seq', 'ctx'))]
    all_gather x1 -> x0, blocking collectives: 32.5 us -> none  [prefix(): gathered = jax.tree.map(lambda a: lax.all_gather(a, axis), part)]
    reduce_sum x33 -> x0, other arithmetic: 20 us -> none  [the longest x16 16.2 us: one_block(): local_grad = jnp.sum(decay_piece * lagged[None], axis=2)]
    all_gather x1 -> x0, waiting for transfers between devices: 19.8 us -> none  [prefix(): gathered = jax.tree.map(lambda a: lax.all_gather(a, axis), part)]
  transfers between devices with their start and end apart: 1 -> 0, of which waited for: 1 -> 0; matrix products, arithmetic and copies ran while one was open for 0% -> 0% of each run, Pallas kernels for 0% -> 0%
where the time goes in v1:
time: 58.8 us; the launch traced here: 58.5 us
  Pallas kernels  52 us (88%)
  local copies, waits for them, and re-layouts  5.8 us (10%)
  between operations  0.65 us (1%)
    pallas_call x1, Pallas kernels, local(): pl.pallas_call(functools.partial(body, shards, seqs, chunks), out_shape=(...  52 us
    unnamed x10, local copies, waits for them, and re-layouts  5.8 us

profile of v1, /device:TPU:0, one launch (start us, length us, event | category | flops | bytes accessed | tf_op | source)
XLA Modules:
  0.0 58.5 jit_solution(13632936103456174830)
XLA Ops:
  0.6 0.0 copy-start
  0.6 1.2 %copy-done = bf16[1,128,4096]{2,1,0:T(8,128)(2,1)S(1)} copy-done((bf16[1,128,4096]{2,1,0:T(8,128)(2,1)S(1)}, bf16[1,128,4096]{2,1,0:T(8,128)(2,1)}, u32[]{:S(2)}) %copy-start) | copy-done | bytes 1048600
  1.9 0.0 copy-start.1
  1.9 1.2 %copy-done.1 = bf16[1,128,4096]{2,1,0:T(8,128)(2,1)S(1)} copy-done((bf16[1,128,4096]{2,1,0:T(8,128)(2,1)S(1)}, bf16[1,128,4096]{2,1,0:T(8,128)(2,1)}, u32[]{:S(2)}) %copy-start.1) | copy-done | bytes 1048600
  3.1 0.0 copy-start.2
  3.1 0.7 %copy-done.2 = f32[16,256]{1,0:T(8,128)S(1)} copy-done((f32[16,256]{1,0:T(8,128)S(1)}, f32[16,256]{1,0:T(8,128)}, u32[]{:S(2)}) %copy-start.2) | copy-done | bytes 16408
  3.8 0.0 copy-start.3
  3.8 0.7 %copy-done.3 = f32[16,256]{1,0:T(8,128)S(1)} copy-done((f32[16,256]{1,0:T(8,128)S(1)}, f32[16,256]{1,0:T(8,128)}, u32[]{:S(2)}) %copy-start.3) | copy-done | bytes 16408
  4.5 52.0 %shard_map.59 = (f32[128,4096]{1,0:T(8,128)S(1)}, f32[16,256]{1,0:T(8,128)S(1)}) custom-call(bf16[128,4096]{1,0:T(8,128)(2,1)S(1)} %bitcast.4, bf16[128,4096]{1,0:T(8,128)(2,1)S(1)} %bitcast.5, f32[16,256]{1,0:T(8,128)S(1)} %copy-done.2, f32[16,256]{1,0:T(8,128)S(1)} %copy-done.3), custom_call_target="tpu_custom_call" | custom-call | tf_op jit(solution)/shard_map/pallas_call | solution.py:316
  56.5 1.3 %copy.8 = f32[1,128,4096]{2,1,0:T(8,128)} copy(f32[1,128,4096]{2,1,0:T(8,128)S(1)} %bitcast.3) | data formatting | bytes 4194304
  57.9 0.6 %copy.9 = f32[16,256]{1,0:T(8,128)} copy(f32[16,256]{1,0:T(8,128)S(1)} %get-tuple-element.9) | data formatting | bytes 32768
Async XLA Ops:
  0.6 1.2 %copy-start = (bf16[1,128,4096]{2,1,0:T(8,128)(2,1)S(1)}, bf16[1,128,4096]{2,1,0:T(8,128)(2,1)}, u32[]{:S(2)}) copy-start(bf16[1,128,4096]{2,1,0:T(8,128)(2,1)} %param.4) | copy-start | bytes 3145732
  1.9 1.2 %copy-start.1 = (bf16[1,128,4096]{2,1,0:T(8,128)(2,1)S(1)}, bf16[1,128,4096]{2,1,0:T(8,128)(2,1)}, u32[]{:S(2)}) copy-start(bf16[1,128,4096]{2,1,0:T(8,128)(2,1)} %param.5) | copy-start | bytes 3145732
  3.1 0.7 %copy-start.2 = (f32[16,256]{1,0:T(8,128)S(1)}, f32[16,256]{1,0:T(8,128)}, u32[]{:S(2)}) copy-start(f32[16,256]{1,0:T(8,128)} %res_ref.1) | copy-start | bytes 49156
  3.8 0.7 %copy-start.3 = (f32[16,256]{1,0:T(8,128)S(1)}, f32[16,256]{1,0:T(8,128)}, u32[]{:S(2)}) copy-start(f32[16,256]{1,0:T(8,128)} %rate_ref.1) | copy-start | bytes 49156

commit v2 on v1

--- a/solution.py
+++ b/solution.py
@@ -29,7 +29,8 @@
 
 
 def body(
-    shards, seqs, chunks, grad_ref, in_ref, res_ref, rate_ref, out_ref, total_ref,
+    shards, seqs, chunks, grad_hbm, in_hbm, res_hbm, rate_hbm, out_ref, total_ref,
+    grad_ref, in_ref, res_ref, rate_ref, small_sem, grad_sem, in_sem,
     own, pair, joined, incoming, outgoing, decay_pow, decay, tail_high, tail_low, tail, lag_sums,
     partial, from_seq, seq_sum, from_ctx,
     pair_send, pair_recv, chain_send, chain_recv, seq_send, seq_recv, ctx_send, ctx_recv,
@@ -46,6 +47,24 @@
     stacked = tile_groups * modes
     pairs = shards // 2
 
+    span = width // chunks
+    rate_copy = pltpu.make_async_copy(rate_hbm, rate_ref, small_sem.at[0])
+    res_copy = pltpu.make_async_copy(res_hbm, res_ref, small_sem.at[1])
+    in_copy = pltpu.make_async_copy(in_hbm, in_ref, in_sem)
+    grad_copies = [
+        pltpu.make_async_copy(
+            grad_hbm.at[:, q * span : (q + 1) * span],
+            grad_ref.at[:, q * span : (q + 1) * span],
+            grad_sem.at[q],
+        )
+        for q in range(chunks)
+    ]
+    rate_copy.start()
+    for copy in grad_copies:
+        copy.start()
+    in_copy.start()
+    res_copy.start()
+
     me = lax.axis_index("ctx")
     my_seq = lax.axis_index("seq")
     upper = me % 2
@@ -91,7 +110,10 @@
             device_id={"ctx": lax.rem(me + shards - 2, shards)}, device_id_type=MESH,
         )
 
+    rate_copy.wait()
     for q in range(chunks):
+        grad_copies[q].wait()
+
         def summarize(step, carry, q=q):
             index = q * chunk_tiles + step
             rates = rolled(rate_ref[...], index)
@@ -115,6 +137,9 @@
             pl.semaphore_wait(barrier, shards - 1 + seqs - 1)
         pair_copy(q).start()
 
+    in_copy.wait()
+    res_copy.wait()
+
     def exchange(step):
         @pl.when(step < chunks)
         def _():
@@ -148,12 +173,22 @@
     steps = chunks + pairs - 1
     per_step = max(1, tiles // steps)
 
-    half_lane_group = lax.broadcasted_iota(jnp.int32, (rows, half), 1) // per_group
+    sub = min(32, rows)
+    subs = rows // sub
+    sub_lane_group = lax.broadcasted_iota(jnp.int32, (sub, half), 1) // per_group
+    folded_group = lax.rem(
+        lax.broadcasted_iota(jnp.int32, (sub, subs * half), 1), half
+    ) // per_group
     row_of = lax.broadcasted_iota(jnp.int32, (rows, rows), 0)
     col_of = lax.broadcasted_iota(jnp.int32, (rows, rows), 1)
-    causal = col_of >= row_of
-    inside = col_of <= row_of
-    reverse = jnp.where(row_of + col_of == rows - 1, 1.0, 0.0).astype(BF16)
+    sub_row = lax.broadcasted_iota(jnp.int32, (sub, rows), 0)
+    sub_col = lax.broadcasted_iota(jnp.int32, (sub, rows), 1)
+    causal = sub_col >= sub_row
+    inside = sub_col <= rows - sub + sub_row
+    mirrored = (row_of // sub == col_of // sub) & (
+        lax.rem(row_of, sub) + lax.rem(col_of, sub) == sub - 1
+    )
+    reverse = jnp.where(mirrored, 1.0, 0.0).astype(BF16)
     group_lane = lax.broadcasted_iota(jnp.int32, (modes, groups), 1)
     amplitude = res_ref[...] * jnp.sqrt(one_minus_exp(2.0 * rate_ref[...]) * (1.0 / modes))
     lag_sums[...] = jnp.zeros_like(lag_sums)
@@ -168,32 +203,53 @@
             where_half = lanes(index * (tile // half) + part, half)
             grads = grad_ref[:, where_half]
             ins = dot(reverse, in_ref[:, where_half]).astype(BF16)
-            doubled = jnp.concatenate([grads, grads], axis=0)
-            result = jnp.zeros((rows, half), F32)
+            shifted = jnp.concatenate(
+                [grads]
+                + [
+                    jnp.concatenate(
+                        [grads[r * sub :], jnp.zeros((r * sub, half), BF16)], axis=0
+                    )
+                    for r in range(1, subs)
+                ],
+                axis=1,
+            )
+            folded = jnp.concatenate([ins[r * sub : (r + 1) * sub] for r in range(subs)], axis=1)
+            filters, masked, kept = [], [], []
             for g8 in range(half_groups):
                 g = part * half_groups + g8
                 rate = rates[:, g : g + 1]
                 amp = amps[:, g : g + 1]
                 decays = decay[pl.ds(pl.multiple_of(index * stacked + g * modes, modes), modes), :]
+                kept.append(decays)
                 filt = jnp.sum(amp * decays, axis=0, keepdims=True)
-                shifted = pltpu.roll(
-                    jnp.broadcast_to(filt, (rows, rows)), 0, 1, stride=1, stride_axis=0
+                toeplitz = pltpu.roll(
+                    jnp.broadcast_to(filt, (sub, rows)), 0, 1, stride=1, stride_axis=0
                 )
-                high, low = split(jnp.where(causal, shifted, 0.0))
-                wide = dot(jnp.concatenate([high, low], axis=1), doubled)
-                result = jnp.where(half_lane_group == g8, wide, result)
-                masked = jnp.where(half_lane_group == g8, ins, jnp.zeros_like(ins))
-                products = lax.dot_general(
-                    masked, grads, (((1,), (1,)), ((), ())), preferred_element_type=F32
-                )
-                skewed = pltpu.roll(products, 1, 1, stride=1, stride_axis=0)
-                lagged = jnp.sum(jnp.where(inside, skewed, 0.0), axis=0, keepdims=True)
-                value = jnp.sum(decays * lagged, axis=1, keepdims=True)
-                sums = jnp.where(group_lane == index * tile_groups + g, value, sums)
+                high, low = split(jnp.where(causal, toeplitz, 0.0))
+                filters.append(jnp.concatenate([high, low], axis=1))
+                masked.append(jnp.where(folded_group == g8, folded, jnp.zeros_like(folded)))
                 remaining = jnp.exp(-rate * behind)
                 tails.append(remaining)
                 weights.append(amp * remaining)
-            out_ref[:, where_half] = result
+            wide = dot(jnp.concatenate(filters, axis=0), jnp.concatenate([shifted, shifted], axis=0))
+            for r in range(subs):
+                result = jnp.zeros((sub, half), F32)
+                for g8 in range(half_groups):
+                    piece = wide[g8 * sub : (g8 + 1) * sub, r * half : (r + 1) * half]
+                    result = jnp.where(sub_lane_group == g8, piece, result)
+                out_ref[r * sub : (r + 1) * sub, where_half] = result
+            products = lax.dot_general(
+                jnp.concatenate(masked, axis=0), shifted, (((1,), (1,)), ((), ())),
+                preferred_element_type=F32,
+            )
+            for g8 in range(half_groups):
+                g = part * half_groups + g8
+                skewed = pltpu.roll(
+                    products[g8 * sub : (g8 + 1) * sub], rows + 1 - sub, 1, stride=1, stride_axis=0
+                )
+                lagged = jnp.sum(jnp.where(inside, skewed, 0.0), axis=0, keepdims=True)
+                value = jnp.sum(kept[g8] * lagged, axis=1, keepdims=True)
+                sums = jnp.where(group_lane == index * tile_groups + g, value, sums)
         lag_sums[...] = sums
         high, low = split(jnp.concatenate(tails, axis=0))
         ins = in_ref[:, lanes(index, tile)]
@@ -249,15 +305,18 @@
     def carry_in(index, carry):
         q, inner = index // chunk_tiles, lax.rem(index, chunk_tiles)
         entry = incoming[q, :, lanes(inner, tile)]
-        blocks = jnp.concatenate(
-            [jnp.where(lane_group == g, entry, 0.0) for g in range(tile_groups)], axis=0
-        )
-        high, low = split(blocks)
+        high, low = split(entry)
+
+        def blocks(value):
+            return jnp.concatenate(
+                [jnp.where(lane_group == g, value, jnp.zeros_like(value)) for g in range(tile_groups)],
+                axis=0,
+            )
+
         left = tail_high[index]
-        out_ref[:, lanes(index, tile)] += dot(
-            jnp.concatenate([left, left, tail_low[index]], axis=1),
-            jnp.concatenate([high, low, high], axis=0),
-        )
+        both = dot(jnp.concatenate([left, tail_low[index]], axis=0), blocks(high))
+        rest = dot(left, blocks(low))
+        out_ref[:, lanes(index, tile)] += both[:rows] + both[rows:] + rest
         return carry
 
     lax.fori_loop(0, tiles // 2, carry_in, 0)
@@ -319,9 +378,11 @@
             jax.ShapeDtypeStruct((rows, width), F32),
             jax.ShapeDtypeStruct(small, F32),
         ),
-        in_specs=[vmem] * 4,
+        in_specs=[pl.BlockSpec(memory_space=pltpu.HBM)] * 4,
         out_specs=(vmem, vmem),
         scratch_shapes=[
+            pltpu.VMEM((rows, width), BF16), pltpu.VMEM((rows, width), BF16),
+            pltpu.VMEM(small, F32), pltpu.VMEM(small, F32), dma((2,)), dma((chunks,)), dma,
             states, states, states, states, states, states,
             pltpu.VMEM((groups * modes, rows), F32),
             pltpu.VMEM((width // tile, rows, tile // (width // groups) * modes), BF16),

time: 58.8 us -> 45.3 us (0.77)
  Pallas kernels: 52 us -> 38.5 us
    pallas_call x1, Pallas kernels: 52 us -> 38.5 us  [local(): pl.pallas_call(functools.partial(body, shards, seqs, chunks), out_shape=(...]
where the time goes in v2:
time: 45.3 us; the launch traced here: 45 us
  Pallas kernels  38.5 us (85%)
  local copies, waits for them, and re-layouts  5.8 us (13%)
  between operations  0.65 us (1%)
    pallas_call x1, Pallas kernels, local(): pl.pallas_call(functools.partial(body, shards, seqs, chunks), out_shape=(...  38.5 us
    unnamed x10, local copies, waits for them, and re-layouts  5.8 us

profile of v2, /device:TPU:0, one launch (start us, length us, event | category | flops | bytes accessed | tf_op | source)
XLA Modules:
  0.0 45.0 jit_solution(3514104413115973484)
XLA Ops:
  0.6 0.0 copy-start
  0.6 1.2 %copy-done = bf16[1,128,4096]{2,1,0:T(8,128)(2,1)S(1)} copy-done((bf16[1,128,4096]{2,1,0:T(8,128)(2,1)S(1)}, bf16[1,128,4096]{2,1,0:T(8,128)(2,1)}, u32[]{:S(2)}) %copy-start) | copy-done | bytes 1048600
  1.9 0.0 copy-start.1
  1.9 1.2 %copy-done.1 = bf16[1,128,4096]{2,1,0:T(8,128)(2,1)S(1)} copy-done((bf16[1,128,4096]{2,1,0:T(8,128)(2,1)S(1)}, bf16[1,128,4096]{2,1,0:T(8,128)(2,1)}, u32[]{:S(2)}) %copy-start.1) | copy-done | bytes 1048600
  3.1 0.0 copy-start.2
  3.1 0.7 %copy-done.2 = f32[16,256]{1,0:T(8,128)S(1)} copy-done((f32[16,256]{1,0:T(8,128)S(1)}, f32[16,256]{1,0:T(8,128)}, u32[]{:S(2)}) %copy-start.2) | copy-done | bytes 16408
  3.8 0.0 copy-start.3
  3.8 0.7 %copy-done.3 = f32[16,256]{1,0:T(8,128)S(1)} copy-done((f32[16,256]{1,0:T(8,128)S(1)}, f32[16,256]{1,0:T(8,128)}, u32[]{:S(2)}) %copy-start.3) | copy-done | bytes 16408
  4.5 38.5 %shard_map.59 = (f32[128,4096]{1,0:T(8,128)S(1)}, f32[16,256]{1,0:T(8,128)S(1)}) custom-call(bf16[128,4096]{1,0:T(8,128)(2,1)S(1)} %bitcast.4, bf16[128,4096]{1,0:T(8,128)(2,1)S(1)} %bitcast.5, f32[16,256]{1,0:T(8,128)S(1)} %copy-done.2, f32[16,256]{1,0:T(8,128)S(1)} %copy-done.3), custom_call_target="tpu_custom_call" | custom-call | tf_op jit(solution)/shard_map/pallas_call | solution.py:375
  43.1 1.3 %copy.8 = f32[1,128,4096]{2,1,0:T(8,128)} copy(f32[1,128,4096]{2,1,0:T(8,128)S(1)} %bitcast.3) | data formatting | bytes 4194304
  44.4 0.6 %copy.9 = f32[16,256]{1,0:T(8,128)} copy(f32[16,256]{1,0:T(8,128)S(1)} %get-tuple-element.9) | data formatting | bytes 32768
Async XLA Ops:
  0.6 1.2 %copy-start = (bf16[1,128,4096]{2,1,0:T(8,128)(2,1)S(1)}, bf16[1,128,4096]{2,1,0:T(8,128)(2,1)}, u32[]{:S(2)}) copy-start(bf16[1,128,4096]{2,1,0:T(8,128)(2,1)} %param.4) | copy-start | bytes 3145732
  1.9 1.2 %copy-start.1 = (bf16[1,128,4096]{2,1,0:T(8,128)(2,1)S(1)}, bf16[1,128,4096]{2,1,0:T(8,128)(2,1)}, u32[]{:S(2)}) copy-start(bf16[1,128,4096]{2,1,0:T(8,128)(2,1)} %param.5) | copy-start | bytes 3145732
  3.1 0.7 %copy-start.2 = (f32[16,256]{1,0:T(8,128)S(1)}, f32[16,256]{1,0:T(8,128)}, u32[]{:S(2)}) copy-start(f32[16,256]{1,0:T(8,128)} %res_hbm.1) | copy-start | bytes 49156
  3.8 0.7 %copy-start.3 = (f32[16,256]{1,0:T(8,128)S(1)}, f32[16,256]{1,0:T(8,128)}, u32[]{:S(2)}) copy-start(f32[16,256]{1,0:T(8,128)} %rate_hbm.1) | copy-start | bytes 49156

commit v3 on v2

--- a/solution.py
+++ b/solution.py
@@ -29,8 +29,8 @@
 
 
 def body(
-    shards, seqs, chunks, grad_hbm, in_hbm, res_hbm, rate_hbm, out_ref, total_ref,
-    grad_ref, in_ref, res_ref, rate_ref, small_sem, grad_sem, in_sem,
+    shards, seqs, chunks, grad_hbm, in_hbm, res_hbm, rate_hbm, out_hbm, total_ref,
+    grad_ref, in_ref, res_ref, rate_ref, out_ref, small_sem, grad_sem, in_sem, out_sem,
     own, pair, joined, incoming, outgoing, decay_pow, decay, tail_high, tail_low, tail, lag_sums,
     partial, from_seq, seq_sum, from_ctx,
     pair_send, pair_recv, chain_send, chain_recv, seq_send, seq_recv, ctx_send, ctx_recv,
@@ -132,7 +132,7 @@
             decay_pow[q, :, lanes(step, tile)] = jnp.exp(-float(rows) * spread)
             return carry
 
-        lax.fori_loop(0, chunk_tiles, summarize, 0)
+        lax.fori_loop(0, chunk_tiles, summarize, 0, unroll=True)
         if q == 0:
             pl.semaphore_wait(barrier, shards - 1 + seqs - 1)
         pair_copy(q).start()
@@ -259,13 +259,17 @@
         tail_high[index] = high
         tail_low[index] = low
 
-        @pl.when(lax.rem(index, per_step) == per_step - 1)
-        def _():
-            exchange(index // per_step)
-
         return carry
 
-    lax.fori_loop(0, tiles, convolve, 0)
+    def advance(step, carry):
+        for inner in range(per_step):
+            convolve(step * per_step + inner, 0)
+        exchange(step)
+        return carry
+
+    lax.fori_loop(0, tiles // per_step, advance, 0)
+    for index in range(tiles // per_step * per_step, tiles):
+        convolve(index, 0)
     for step in range(tiles // per_step, steps):
         exchange(step)
 
@@ -285,7 +289,7 @@
         found = dot(jnp.concatenate([high, middle, low], axis=0), member)
         return sums + found[:modes] + found[modes : 2 * modes] + found[2 * modes :]
 
-    partial[...] = lax.fori_loop(0, tiles, enter, lag_sums[...])
+    partial[...] = lax.fori_loop(0, tiles, enter, lag_sums[...], unroll=4)
 
     def seq_copy(offset):
         return pltpu.make_async_remote_copy(
@@ -319,7 +323,19 @@
         out_ref[:, lanes(index, tile)] += both[:rows] + both[rows:] + rest
         return carry
 
-    lax.fori_loop(0, tiles // 2, carry_in, 0)
+    def out_copy(q):
+        return pltpu.make_async_copy(
+            out_ref.at[:, q * span : (q + 1) * span],
+            out_hbm.at[:, q * span : (q + 1) * span],
+            out_sem.at[q],
+        )
+
+    def finish(q):
+        lax.fori_loop(q * chunk_tiles, (q + 1) * chunk_tiles, carry_in, 0, unroll=True)
+        out_copy(q).start()
+
+    for q in range(chunks // 2):
+        finish(q)
     for offset in range(1, seqs):
         seq_copy(offset).wait_recv()
 
@@ -337,7 +353,8 @@
     seq_sum[...] = ordered(partial[...], from_seq, my_seq, seqs)
     for offset in range(1, shards):
         ctx_copy(offset).start()
-    lax.fori_loop(tiles // 2, tiles, carry_in, 0)
+    for q in range(chunks // 2, chunks):
+        finish(q)
     for offset in range(1, shards):
         ctx_copy(offset).wait_recv()
 
@@ -351,6 +368,7 @@
     total_ref[...] = total * jnp.sqrt(one_minus_exp(2.0 * rate_ref[...]) * scale)
 
     for q in range(chunks):
+        out_copy(q).wait()
         pair_copy(q).wait_send()
         if pairs > 1:
             @pl.when(place > 0)
@@ -379,10 +397,11 @@
             jax.ShapeDtypeStruct(small, F32),
         ),
         in_specs=[pl.BlockSpec(memory_space=pltpu.HBM)] * 4,
-        out_specs=(vmem, vmem),
+        out_specs=(pl.BlockSpec(memory_space=pltpu.HBM), vmem),
         scratch_shapes=[
             pltpu.VMEM((rows, width), BF16), pltpu.VMEM((rows, width), BF16),
-            pltpu.VMEM(small, F32), pltpu.VMEM(small, F32), dma((2,)), dma((chunks,)), dma,
+            pltpu.VMEM(small, F32), pltpu.VMEM(small, F32), pltpu.VMEM((rows, width), F32),
+            dma((2,)), dma((chunks,)), dma, dma((chunks,)),
             states, states, states, states, states, states,
             pltpu.VMEM((groups * modes, rows), F32),
             pltpu.VMEM((width // tile, rows, tile // (width // groups) * modes), BF16),
@@ -397,7 +416,7 @@
             dma((seqs - 1,)), dma((seqs - 1,)), dma((shards - 1,)), dma((shards - 1,)),
         ],
         compiler_params=pltpu.CompilerParams(
-            collective_id=0, has_side_effects=True, vmem_limit_bytes=40 * 1024 * 1024
+            collective_id=0, has_side_effects=True, vmem_limit_bytes=63 * 1024 * 1024
         ),
     )(grad_out[0], inputs[0], residues, rates)
     return grad_in[None], total

time: 45.3 us -> 40.6 us (0.90)
  Pallas kernels: 38.5 us -> 36 us
  local copies, waits for them, and re-layouts: 5.8 us -> 3.73 us
    pallas_call x1, Pallas kernels: 38.5 us -> 36 us  [local(): pl.pallas_call(functools.partial(body, shards, seqs, chunks), out_shape=(...]
    unnamed x10 -> x4, local copies, waits for them, and re-layouts: 5.8 us -> 3.73 us
where the time goes in v3:
time: 40.6 us; the launch traced here: 40.4 us
  Pallas kernels  36 us (89%)
  local copies, waits for them, and re-layouts  3.73 us (9%)
  between operations  0.65 us (2%)
    pallas_call x1, Pallas kernels, local(): pl.pallas_call(functools.partial(body, shards, seqs, chunks), out_shape=(...  36 us
    unnamed x4, local copies, waits for them, and re-layouts  3.73 us

profile of v3, /device:TPU:0, one launch (start us, length us, event | category | flops | bytes accessed | tf_op | source)
XLA Modules:
  0.0 40.4 jit_solution(10926409763613726517)
XLA Ops:
  0.6 36.0 %shard_map.59 = (f32[128,4096]{1,0:T(8,128)}, f32[16,256]{1,0:T(8,128)}) custom-call(bf16[128,4096]{1,0:T(8,128)(2,1)} %bitcast.4, bf16[128,4096]{1,0:T(8,128)(2,1)} %bitcast.5, f32[16,256]{1,0:T(8,128)} %res_hbm.1, f32[16,256]{1,0:T(8,128)} %rate_hbm.1), custom_call_target="tpu_custom_call" | custom-call | tf_op jit(solution)/shard_map/pallas_call | solution.py:393
  36.7 0.0 copy-start
  36.7 3.1 %copy.8 = f32[1,128,4096]{2,1,0:T(8,128)} copy(f32[1,128,4096]{2,1,0:T(8,128)} %bitcast.3) | data formatting | bytes 4194304
  39.8 0.0 copy-done
  39.8 0.6 %copy.9 = f32[16,256]{1,0:T(8,128)} copy(f32[16,256]{1,0:T(8,128)S(1)} %copy-done) | data formatting | bytes 32768
Async XLA Ops:
  36.7 3.1 %copy-start = (f32[16,256]{1,0:T(8,128)S(1)}, f32[16,256]{1,0:T(8,128)}, u32[]{:S(2)}) copy-start(f32[16,256]{1,0:T(8,128)} %get-tuple-element.9) | copy-start | bytes 49156

commit v4 on v3

--- a/solution.py
+++ b/solution.py
@@ -176,9 +176,11 @@
     sub = min(32, rows)
     subs = rows // sub
     sub_lane_group = lax.broadcasted_iota(jnp.int32, (sub, half), 1) // per_group
-    folded_group = lax.rem(
-        lax.broadcasted_iota(jnp.int32, (sub, subs * half), 1), half
-    ) // per_group
+    folded_masks = []
+    for g in range(half_groups):
+        mask = jnp.where(sub_lane_group == g, 1.0, 0.0).astype(BF16)
+        folded_masks.append(jnp.concatenate([mask] * subs, axis=1))
+    tile_masks = [jnp.where(lane_group == g, 1.0, 0.0).astype(BF16) for g in range(tile_groups)]
     row_of = lax.broadcasted_iota(jnp.int32, (rows, rows), 0)
     col_of = lax.broadcasted_iota(jnp.int32, (rows, rows), 1)
     sub_row = lax.broadcasted_iota(jnp.int32, (sub, rows), 0)
@@ -193,7 +195,20 @@
     amplitude = res_ref[...] * jnp.sqrt(one_minus_exp(2.0 * rate_ref[...]) * (1.0 / modes))
     lag_sums[...] = jnp.zeros_like(lag_sums)
 
-    def convolve(index, carry):
+    def folded_rows(grads):
+        return jnp.concatenate(
+            [grads]
+            + [
+                jnp.concatenate([grads[r * sub :], jnp.zeros((r * sub, half), BF16)], axis=0)
+                for r in range(1, subs)
+            ],
+            axis=1,
+        )
+
+    def group_decays(index, g):
+        return decay[pl.ds(pl.multiple_of(index * stacked + g * modes, modes), modes), :]
+
+    def correlate(index):
         rates = rolled(rate_ref[...], index)
         amps = rolled(amplitude, index)
         tails = []
@@ -201,46 +216,12 @@
         sums = lag_sums[...]
         for part in range(tile // half):
             where_half = lanes(index * (tile // half) + part, half)
-            grads = grad_ref[:, where_half]
+            shifted = folded_rows(grad_ref[:, where_half])
             ins = dot(reverse, in_ref[:, where_half]).astype(BF16)
-            shifted = jnp.concatenate(
-                [grads]
-                + [
-                    jnp.concatenate(
-                        [grads[r * sub :], jnp.zeros((r * sub, half), BF16)], axis=0
-                    )
-                    for r in range(1, subs)
-                ],
-                axis=1,
-            )
             folded = jnp.concatenate([ins[r * sub : (r + 1) * sub] for r in range(subs)], axis=1)
-            filters, masked, kept = [], [], []
-            for g8 in range(half_groups):
-                g = part * half_groups + g8
-                rate = rates[:, g : g + 1]
-                amp = amps[:, g : g + 1]
-                decays = decay[pl.ds(pl.multiple_of(index * stacked + g * modes, modes), modes), :]
-                kept.append(decays)
-                filt = jnp.sum(amp * decays, axis=0, keepdims=True)
-                toeplitz = pltpu.roll(
-                    jnp.broadcast_to(filt, (sub, rows)), 0, 1, stride=1, stride_axis=0
-                )
-                high, low = split(jnp.where(causal, toeplitz, 0.0))
-                filters.append(jnp.concatenate([high, low], axis=1))
-                masked.append(jnp.where(folded_group == g8, folded, jnp.zeros_like(folded)))
-                remaining = jnp.exp(-rate * behind)
-                tails.append(remaining)
-                weights.append(amp * remaining)
-            wide = dot(jnp.concatenate(filters, axis=0), jnp.concatenate([shifted, shifted], axis=0))
-            for r in range(subs):
-                result = jnp.zeros((sub, half), F32)
-                for g8 in range(half_groups):
-                    piece = wide[g8 * sub : (g8 + 1) * sub, r * half : (r + 1) * half]
-                    result = jnp.where(sub_lane_group == g8, piece, result)
-                out_ref[r * sub : (r + 1) * sub, where_half] = result
             products = lax.dot_general(
-                jnp.concatenate(masked, axis=0), shifted, (((1,), (1,)), ((), ())),
-                preferred_element_type=F32,
+                jnp.concatenate([folded * mask for mask in folded_masks], axis=0),
+                shifted, (((1,), (1,)), ((), ())), preferred_element_type=F32,
             )
             for g8 in range(half_groups):
                 g = part * half_groups + g8
@@ -248,8 +229,11 @@
                     products[g8 * sub : (g8 + 1) * sub], rows + 1 - sub, 1, stride=1, stride_axis=0
                 )
                 lagged = jnp.sum(jnp.where(inside, skewed, 0.0), axis=0, keepdims=True)
-                value = jnp.sum(kept[g8] * lagged, axis=1, keepdims=True)
+                value = jnp.sum(group_decays(index, g) * lagged, axis=1, keepdims=True)
                 sums = jnp.where(group_lane == index * tile_groups + g, value, sums)
+                remaining = jnp.exp(-rates[:, g : g + 1] * behind)
+                tails.append(remaining)
+                weights.append(amps[:, g : g + 1] * remaining)
         lag_sums[...] = sums
         high, low = split(jnp.concatenate(tails, axis=0))
         ins = in_ref[:, lanes(index, tile)]
@@ -259,17 +243,48 @@
         tail_high[index] = high
         tail_low[index] = low
 
-        return carry
+    def convolve(index):
+        q, inner = index // chunk_tiles, lax.rem(index, chunk_tiles)
+        amps = rolled(amplitude, index)
+        high, low = split(incoming[q, :, lanes(inner, tile)])
+        left = tail_high[index]
+        both = dot(
+            jnp.concatenate([left, tail_low[index]], axis=0),
+            jnp.concatenate([high * mask for mask in tile_masks], axis=0),
+        )
+        rest = dot(left, jnp.concatenate([low * mask for mask in tile_masks], axis=0))
+        entered = both[:rows] + both[rows:] + rest
+        for part in range(tile // half):
+            where_half = lanes(index * (tile // half) + part, half)
+            shifted = folded_rows(grad_ref[:, where_half])
+            filters = []
+            for g8 in range(half_groups):
+                g = part * half_groups + g8
+                filt = jnp.sum(amps[:, g : g + 1] * group_decays(index, g), axis=0, keepdims=True)
+                toeplitz = pltpu.roll(
+                    jnp.broadcast_to(filt, (sub, rows)), 0, 1, stride=1, stride_axis=0
+                )
+                high, low = split(jnp.where(causal, toeplitz, 0.0))
+                filters.append(jnp.concatenate([high, low], axis=1))
+            wide = dot(jnp.concatenate(filters, axis=0), jnp.concatenate([shifted, shifted], axis=0))
+            for r in range(subs):
+                result = wide[:sub, r * half : (r + 1) * half]
+                for g8 in range(1, half_groups):
+                    piece = wide[g8 * sub : (g8 + 1) * sub, r * half : (r + 1) * half]
+                    result = jnp.where(sub_lane_group == g8, piece, result)
+                out_ref[r * sub : (r + 1) * sub, where_half] = (
+                    result + entered[r * sub : (r + 1) * sub, part * half : (part + 1) * half]
+                )
 
     def advance(step, carry):
         for inner in range(per_step):
-            convolve(step * per_step + inner, 0)
+            correlate(step * per_step + inner)
         exchange(step)
         return carry
 
     lax.fori_loop(0, tiles // per_step, advance, 0)
     for index in range(tiles // per_step * per_step, tiles):
-        convolve(index, 0)
+        correlate(index)
     for step in range(tiles // per_step, steps):
         exchange(step)
 
@@ -306,23 +321,6 @@
     for offset in range(1, seqs):
         seq_copy(offset).start()
 
-    def carry_in(index, carry):
-        q, inner = index // chunk_tiles, lax.rem(index, chunk_tiles)
-        entry = incoming[q, :, lanes(inner, tile)]
-        high, low = split(entry)
-
-        def blocks(value):
-            return jnp.concatenate(
-                [jnp.where(lane_group == g, value, jnp.zeros_like(value)) for g in range(tile_groups)],
-                axis=0,
-            )
-
-        left = tail_high[index]
-        both = dot(jnp.concatenate([left, tail_low[index]], axis=0), blocks(high))
-        rest = dot(left, blocks(low))
-        out_ref[:, lanes(index, tile)] += both[:rows] + both[rows:] + rest
-        return carry
-
     def out_copy(q):
         return pltpu.make_async_copy(
             out_ref.at[:, q * span : (q + 1) * span],
@@ -330,8 +328,15 @@
             out_sem.at[q],
         )
 
+    unrolled = 2 if chunk_tiles % 2 == 0 else 1
+
     def finish(q):
-        lax.fori_loop(q * chunk_tiles, (q + 1) * chunk_tiles, carry_in, 0, unroll=True)
+        def pieces(step, carry):
+            for inner in range(unrolled):
+                convolve(q * chunk_tiles + step * unrolled + inner)
+            return carry
+
+        lax.fori_loop(0, chunk_tiles // unrolled, pieces, 0)
         out_copy(q).start()
 
     for q in range(chunks // 2):
@@ -364,8 +369,7 @@
         return added + jnp.where(offset == 0, seq_sum[...], from_ctx[slot])
 
     total = lax.fori_loop(0, shards, gather_sum, jnp.zeros((modes, groups), F32))
-    scale = 1.0 / float(seqs * shards * rows * per_group)
-    total_ref[...] = total * jnp.sqrt(one_minus_exp(2.0 * rate_ref[...]) * scale)
+    total_ref[...] = total
 
     for q in range(chunks):
         out_copy(q).wait()
@@ -378,6 +382,11 @@
         seq_copy(offset).wait_send()
     for offset in range(1, shards):
         ctx_copy(offset).wait_send()
+
+
+def write(count, grad_ref, sum_ref, rate_ref, out_ref, total_ref):
+    out_ref[...] = grad_ref[...]
+    total_ref[...] = sum_ref[...] * jnp.sqrt(one_minus_exp(2.0 * rate_ref[...]) * (1.0 / count))
 
 
 def local(shards, seqs, grad_out, inputs, residues, rates):
@@ -419,6 +428,17 @@
             collective_id=0, has_side_effects=True, vmem_limit_bytes=63 * 1024 * 1024
         ),
     )(grad_out[0], inputs[0], residues, rates)
+    span = width // 8
+    piece = pl.BlockSpec((rows, span), lambda i: (0, i))
+    whole = pl.BlockSpec(small, lambda i: (0, 0))
+    grad_in, total = pl.pallas_call(
+        functools.partial(write, float(seqs * shards * rows * (width // groups))),
+        grid=(width // span,),
+        out_shape=(jax.ShapeDtypeStruct((rows, width), F32), jax.ShapeDtypeStruct(small, F32)),
+        in_specs=[piece, whole, whole],
+        out_specs=(piece, whole),
+        compiler_params=pltpu.CompilerParams(vmem_limit_bytes=63 * 1024 * 1024),
+    )(grad_in, total, rates)
     return grad_in[None], total
 
 

time: 40.6 us -> 47.3 us (1.17)
  Pallas kernels: 36 us -> 46.4 us
  local copies, waits for them, and re-layouts: 3.73 us -> 0 us
    pallas_call x0 -> x1, Pallas kernels: none -> 5.66 us  [local(): pl.pallas_call(functools.partial(write, float(seqs * shards * rows * (wid...]
    pallas_call x1, Pallas kernels: 36 us -> 40.7 us  [local(): pl.pallas_call(functools.partial(body, shards, seqs, chunks), out_shape=(...]
    unnamed x4 -> x0, local copies, waits for them, and re-layouts: 3.73 us -> none
where the time goes in v4:
time: 47.3 us; the launch traced here: 47 us
  Pallas kernels  46.4 us (98%)
  between operations  0.64 us (1%)
    pallas_call x1, Pallas kernels, local(): pl.pallas_call(functools.partial(body, shards, seqs, chunks), out_shape=(...  40.7 us
    pallas_call x1, Pallas kernels, local(): pl.pallas_call(functools.partial(write, float(seqs * shards * rows * (wid...  5.66 us

profile of v4, /device:TPU:0, one launch (start us, length us, event | category | flops | bytes accessed | tf_op | source)
XLA Modules:
  0.0 47.0 jit_solution(7812961323517722046)
XLA Ops:
  0.6 40.7 %shard_map.59 = (f32[128,4096]{1,0:T(8,128)}, f32[16,256]{1,0:T(8,128)}) custom-call(bf16[128,4096]{1,0:T(8,128)(2,1)} %bitcast.3, bf16[128,4096]{1,0:T(8,128)(2,1)} %bitcast.4, f32[16,256]{1,0:T(8,128)} %res_hbm.1, f32[16,256]{1,0:T(8,128)} %rate_ref.1), custom_call_target="tpu_custom_call" | custom-call | tf_op jit(solution)/shard_map/pallas_call | solution.py:402
  41.4 5.7 %shard_map.60 = (f32[128,4096]{1,0:T(8,128)}, f32[16,256]{1,0:T(8,128)}) custom-call(f32[128,4096]{1,0:T(8,128)} %get-tuple-element.6.grad_ref, f32[16,256]{1,0:T(8,128)} %get-tuple-element.7.sum_ref, f32[16,256]{1,0:T(8,128)} %rate_ref.1), custom_call_target="tpu_custom_call" | custom-call | tf_op jit(solution)/shard_map/pallas_call | solution.py:434

commit v5 on v4

--- a/solution.py
+++ b/solution.py
@@ -96,6 +96,8 @@
         return kept
 
     def lanes(index, size):
+        if isinstance(index, int):
+            return pl.ds(index * size, size)
         return pl.ds(pl.multiple_of(index * size, size), size)
 
     def pair_copy(q):
@@ -171,7 +173,6 @@
                     chain_copy(q).start()
 
     steps = chunks + pairs - 1
-    per_step = max(1, tiles // steps)
 
     sub = min(32, rows)
     subs = rows // sub
@@ -206,7 +207,8 @@
         )
 
     def group_decays(index, g):
-        return decay[pl.ds(pl.multiple_of(index * stacked + g * modes, modes), modes), :]
+        start = index * stacked + g * modes
+        return decay[pl.ds(start if isinstance(start, int) else pl.multiple_of(start, modes), modes), :]
 
     def correlate(index):
         rates = rolled(rate_ref[...], index)
@@ -243,9 +245,8 @@
         tail_high[index] = high
         tail_low[index] = low
 
-    def convolve(index):
+    def carried(index):
         q, inner = index // chunk_tiles, lax.rem(index, chunk_tiles)
-        amps = rolled(amplitude, index)
         high, low = split(incoming[q, :, lanes(inner, tile)])
         left = tail_high[index]
         both = dot(
@@ -253,7 +254,10 @@
             jnp.concatenate([high * mask for mask in tile_masks], axis=0),
         )
         rest = dot(left, jnp.concatenate([low * mask for mask in tile_masks], axis=0))
-        entered = both[:rows] + both[rows:] + rest
+        return both[:rows] + both[rows:] + rest
+
+    def convolve(index, entered=None):
+        amps = rolled(amplitude, index)
         for part in range(tile // half):
             where_half = lanes(index * (tile // half) + part, half)
             shifted = folded_rows(grad_ref[:, where_half])
@@ -272,20 +276,27 @@
                 for g8 in range(1, half_groups):
                     piece = wide[g8 * sub : (g8 + 1) * sub, r * half : (r + 1) * half]
                     result = jnp.where(sub_lane_group == g8, piece, result)
-                out_ref[r * sub : (r + 1) * sub, where_half] = (
-                    result + entered[r * sub : (r + 1) * sub, part * half : (part + 1) * half]
-                )
-
-    def advance(step, carry):
-        for inner in range(per_step):
-            correlate(step * per_step + inner)
+                if entered is not None:
+                    result += entered[r * sub : (r + 1) * sub, part * half : (part + 1) * half]
+                out_ref[r * sub : (r + 1) * sub, where_half] = result
+
+    assert tiles % 4 == 0 and chunks % 2 == 0
+
+    def first(step, carry):
+        for inner in range(2):
+            correlate(step * 2 + inner)
         exchange(step)
         return carry
 
-    lax.fori_loop(0, tiles // per_step, advance, 0)
-    for index in range(tiles // per_step * per_step, tiles):
-        correlate(index)
-    for step in range(tiles // per_step, steps):
+    def second(step, carry):
+        for inner in range(2):
+            convolve(step * 2 + inner)
+        exchange(tiles // 2 + step)
+        return carry
+
+    lax.fori_loop(0, tiles // 2, first, 0)
+    lax.fori_loop(0, tiles // 4, second, 0)
+    for step in range(tiles // 2 + tiles // 4, steps):
         exchange(step)
 
     def enter(index, sums):
@@ -328,18 +339,15 @@
             out_sem.at[q],
         )
 
-    unrolled = 2 if chunk_tiles % 2 == 0 else 1
-
     def finish(q):
-        def pieces(step, carry):
-            for inner in range(unrolled):
-                convolve(q * chunk_tiles + step * unrolled + inner)
-            return carry
-
-        lax.fori_loop(0, chunk_tiles // unrolled, pieces, 0)
+        for index in range(q * chunk_tiles, (q + 1) * chunk_tiles):
+            if index < tiles // 2:
+                out_ref[:, lanes(index, tile)] += carried(index)
+            else:
+                convolve(index, carried(index))
         out_copy(q).start()
 
-    for q in range(chunks // 2):
+    for q in range(chunks // 2, 3 * chunks // 4):
         finish(q)
     for offset in range(1, seqs):
         seq_copy(offset).wait_recv()
@@ -358,7 +366,9 @@
     seq_sum[...] = ordered(partial[...], from_seq, my_seq, seqs)
     for offset in range(1, shards):
         ctx_copy(offset).start()
-    for q in range(chunks // 2, chunks):
+    for q in range(3 * chunks // 4, chunks):
+        finish(q)
+    for q in range(chunks // 2):
         finish(q)
     for offset in range(1, shards):
         ctx_copy(offset).wait_recv()
@@ -369,7 +379,8 @@
         return added + jnp.where(offset == 0, seq_sum[...], from_ctx[slot])
 
     total = lax.fori_loop(0, shards, gather_sum, jnp.zeros((modes, groups), F32))
-    total_ref[...] = total
+    scale = 1.0 / float(seqs * shards * rows * per_group)
+    total_ref[...] = total * jnp.sqrt(one_minus_exp(2.0 * rate_ref[...]) * scale)
 
     for q in range(chunks):
         out_copy(q).wait()
@@ -384,15 +395,10 @@
         ctx_copy(offset).wait_send()
 
 
-def write(count, grad_ref, sum_ref, rate_ref, out_ref, total_ref):
-    out_ref[...] = grad_ref[...]
-    total_ref[...] = sum_ref[...] * jnp.sqrt(one_minus_exp(2.0 * rate_ref[...]) * (1.0 / count))
-
-
 def local(shards, seqs, grad_out, inputs, residues, rates):
     rows, width = grad_out.shape[1:]
     modes, groups = residues.shape
-    chunks = 4
+    chunks = 8
     tile = 256
     chunk_shape = (chunks, modes, width // chunks)
     small = (modes, groups)
@@ -428,17 +434,6 @@
             collective_id=0, has_side_effects=True, vmem_limit_bytes=63 * 1024 * 1024
         ),
     )(grad_out[0], inputs[0], residues, rates)
-    span = width // 8
-    piece = pl.BlockSpec((rows, span), lambda i: (0, i))
-    whole = pl.BlockSpec(small, lambda i: (0, 0))
-    grad_in, total = pl.pallas_call(
-        functools.partial(write, float(seqs * shards * rows * (width // groups))),
-        grid=(width // span,),
-        out_shape=(jax.ShapeDtypeStruct((rows, width), F32), jax.ShapeDtypeStruct(small, F32)),
-        in_specs=[piece, whole, whole],
-        out_specs=(piece, whole),
-        compiler_params=pltpu.CompilerParams(vmem_limit_bytes=63 * 1024 * 1024),
-    )(grad_in, total, rates)
     return grad_in[None], total
 
 

time: 47.3 us -> 52.2 us (1.10)
  local copies, waits for them, and re-layouts: 0 us -> 3.73 us
  Pallas kernels: 46.4 us -> 47.6 us
    pallas_call x1, Pallas kernels: 40.7 us -> 47.6 us  [local(): pl.pallas_call(functools.partial(body, shards, seqs, chunks), out_shape=(...]
    pallas_call x1 -> x0, Pallas kernels: 5.66 us -> none  [local(): pl.pallas_call(functools.partial(write, float(seqs * shards * rows * (wid...]
    unnamed x0 -> x4, local copies, waits for them, and re-layouts: none -> 3.73 us
where the time goes in v5:
time: 52.2 us; the launch traced here: 52 us
  Pallas kernels  47.6 us (91%)
  local copies, waits for them, and re-layouts  3.73 us (7%)
  between operations  0.65 us (1%)
    pallas_call x1, Pallas kernels, local(): pl.pallas_call(functools.partial(body, shards, seqs, chunks), out_shape=(...  47.6 us
    unnamed x4, local copies, waits for them, and re-layouts  3.73 us

profile of v5, /device:TPU:0, one launch (start us, length us, event | category | flops | bytes accessed | tf_op | source)
XLA Modules:
  0.0 52.0 jit_solution(5684164062947623468)
XLA Ops:
  0.6 47.6 %shard_map.59 = (f32[128,4096]{1,0:T(8,128)}, f32[16,256]{1,0:T(8,128)}) custom-call(bf16[128,4096]{1,0:T(8,128)(2,1)} %bitcast.4, bf16[128,4096]{1,0:T(8,128)(2,1)} %bitcast.5, f32[16,256]{1,0:T(8,128)} %res_hbm.1, f32[16,256]{1,0:T(8,128)} %rate_hbm.1), custom_call_target="tpu_custom_call" | custom-call | tf_op jit(solution)/shard_map/pallas_call | solution.py:408
  48.2 0.0 copy-start
  48.3 3.1 %copy.8 = f32[1,128,4096]{2,1,0:T(8,128)} copy(f32[1,128,4096]{2,1,0:T(8,128)} %bitcast.3) | data formatting | bytes 4194304
  51.4 0.0 copy-done
  51.4 0.6 %copy.9 = f32[16,256]{1,0:T(8,128)} copy(f32[16,256]{1,0:T(8,128)S(1)} %copy-done) | data formatting | bytes 32768
Async XLA Ops:
  48.2 3.1 %copy-start = (f32[16,256]{1,0:T(8,128)S(1)}, f32[16,256]{1,0:T(8,128)}, u32[]{:S(2)}) copy-start(f32[16,256]{1,0:T(8,128)} %get-tuple-element.9) | copy-start | bytes 49156

commit v6 on v3

--- a/solution.py
+++ b/solution.py
@@ -51,17 +51,13 @@
     rate_copy = pltpu.make_async_copy(rate_hbm, rate_ref, small_sem.at[0])
     res_copy = pltpu.make_async_copy(res_hbm, res_ref, small_sem.at[1])
     in_copy = pltpu.make_async_copy(in_hbm, in_ref, in_sem)
-    grad_copies = [
-        pltpu.make_async_copy(
-            grad_hbm.at[:, q * span : (q + 1) * span],
-            grad_ref.at[:, q * span : (q + 1) * span],
-            grad_sem.at[q],
-        )
-        for q in range(chunks)
-    ]
+    def grad_copy(q):
+        where = pl.ds(pl.multiple_of(q * span, span), span)
+        return pltpu.make_async_copy(grad_hbm.at[:, where], grad_ref.at[:, where], grad_sem.at[q])
+
     rate_copy.start()
-    for copy in grad_copies:
-        copy.start()
+    for q in range(chunks):
+        grad_copy(q).start()
     in_copy.start()
     res_copy.start()
 
@@ -111,10 +107,10 @@
         )
 
     rate_copy.wait()
-    for q in range(chunks):
-        grad_copies[q].wait()
-
-        def summarize(step, carry, q=q):
+    def summaries(q, carry):
+        grad_copy(q).wait()
+
+        def summarize(step, carry):
             index = q * chunk_tiles + step
             rates = rolled(rate_ref[...], index)
             spread = jnp.zeros((modes, tile), F32)
@@ -133,9 +129,15 @@
             return carry
 
         lax.fori_loop(0, chunk_tiles, summarize, 0, unroll=True)
-        if q == 0:
+
+        @pl.when(q == 0)
+        def _():
             pl.semaphore_wait(barrier, shards - 1 + seqs - 1)
+
         pair_copy(q).start()
+        return carry
+
+    lax.fori_loop(0, chunks, summaries, 0)
 
     in_copy.wait()
     res_copy.wait()
@@ -325,17 +327,19 @@
 
     def out_copy(q):
         return pltpu.make_async_copy(
-            out_ref.at[:, q * span : (q + 1) * span],
-            out_hbm.at[:, q * span : (q + 1) * span],
+            out_ref.at[:, pl.ds(pl.multiple_of(q * span, span), span)],
+            out_hbm.at[:, pl.ds(pl.multiple_of(q * span, span), span)],
             out_sem.at[q],
         )
 
-    def finish(q):
-        lax.fori_loop(q * chunk_tiles, (q + 1) * chunk_tiles, carry_in, 0, unroll=True)
+    def finish(q, carry):
+        lax.fori_loop(
+            0, chunk_tiles, lambda step, c: carry_in(q * chunk_tiles + step, c), 0, unroll=True
+        )
         out_copy(q).start()
-
-    for q in range(chunks // 2):
-        finish(q)
+        return carry
+
+    lax.fori_loop(0, chunks // 2, finish, 0)
     for offset in range(1, seqs):
         seq_copy(offset).wait_recv()
 
@@ -353,8 +357,7 @@
     seq_sum[...] = ordered(partial[...], from_seq, my_seq, seqs)
     for offset in range(1, shards):
         ctx_copy(offset).start()
-    for q in range(chunks // 2, chunks):
-        finish(q)
+    lax.fori_loop(chunks // 2, chunks, finish, 0)
     for offset in range(1, shards):
         ctx_copy(offset).wait_recv()
 

time: 40.6 us -> 40.8 us (level)
  no operation moved by 1% of the time
where the time goes in v6:
time: 40.8 us; the launch traced here: 40.6 us
  Pallas kernels  36.3 us (89%)
  local copies, waits for them, and re-layouts  3.73 us (9%)
  between operations  0.65 us (2%)
    pallas_call x1, Pallas kernels, local(): pl.pallas_call(functools.partial(body, shards, seqs, chunks), out_shape=(...  36.3 us
    unnamed x4, local copies, waits for them, and re-layouts  3.73 us

profile of v6, /device:TPU:0, one launch (start us, length us, event | category | flops | bytes accessed | tf_op | source)
XLA Modules:
  0.0 40.6 jit_solution(7006459898166261846)
XLA Ops:
  0.6 36.3 %shard_map.59 = (f32[128,4096]{1,0:T(8,128)}, f32[16,256]{1,0:T(8,128)}) custom-call(bf16[128,4096]{1,0:T(8,128)(2,1)} %bitcast.4, bf16[128,4096]{1,0:T(8,128)(2,1)} %bitcast.5, f32[16,256]{1,0:T(8,128)} %res_hbm.1, f32[16,256]{1,0:T(8,128)} %rate_hbm.1), custom_call_target="tpu_custom_call" | custom-call | tf_op jit(solution)/shard_map/pallas_call | solution.py:396
  36.9 0.0 copy-start
  36.9 3.1 %copy.8 = f32[1,128,4096]{2,1,0:T(8,128)} copy(f32[1,128,4096]{2,1,0:T(8,128)} %bitcast.3) | data formatting | bytes 4194304
  40.0 0.0 copy-done
  40.0 0.6 %copy.9 = f32[16,256]{1,0:T(8,128)} copy(f32[16,256]{1,0:T(8,128)S(1)} %copy-done) | data formatting | bytes 32768
Async XLA Ops:
  36.9 3.1 %copy-start = (f32[16,256]{1,0:T(8,128)S(1)}, f32[16,256]{1,0:T(8,128)}, u32[]{:S(2)}) copy-start(f32[16,256]{1,0:T(8,128)} %get-tuple-element.9) | copy-start | bytes 49156

commit v7 on v3

--- a/solution.py
+++ b/solution.py
@@ -173,7 +173,7 @@
     steps = chunks + pairs - 1
     per_step = max(1, tiles // steps)
 
-    sub = min(32, rows)
+    sub = min(16, rows)
     subs = rows // sub
     sub_lane_group = lax.broadcasted_iota(jnp.int32, (sub, half), 1) // per_group
     folded_group = lax.rem(

time: 40.6 us -> 38.6 us (0.951)
  Pallas kernels: 36 us -> 34.1 us
    pallas_call x1, Pallas kernels: 36 us -> 34.1 us  [local(): pl.pallas_call(functools.partial(body, shards, seqs, chunks), out_shape=(...]
where the time goes in v7:
time: 38.6 us; the launch traced here: 38.4 us
  Pallas kernels  34.1 us (88%)
  local copies, waits for them, and re-layouts  3.73 us (10%)
  between operations  0.65 us (2%)
    pallas_call x1, Pallas kernels, local(): pl.pallas_call(functools.partial(body, shards, seqs, chunks), out_shape=(...  34.1 us
    unnamed x4, local copies, waits for them, and re-layouts  3.73 us

profile of v7, /device:TPU:0, one launch (start us, length us, event | category | flops | bytes accessed | tf_op | source)
XLA Modules:
  0.0 38.4 jit_solution(6457072007510698355)
XLA Ops:
  0.6 34.1 %shard_map.59 = (f32[128,4096]{1,0:T(8,128)}, f32[16,256]{1,0:T(8,128)}) custom-call(bf16[128,4096]{1,0:T(8,128)(2,1)} %bitcast.4, bf16[128,4096]{1,0:T(8,128)(2,1)} %bitcast.5, f32[16,256]{1,0:T(8,128)} %res_hbm.1, f32[16,256]{1,0:T(8,128)} %rate_hbm.1), custom_call_target="tpu_custom_call" | custom-call | tf_op jit(solution)/shard_map/pallas_call | solution.py:393
  34.7 0.0 copy-start
  34.7 3.1 %copy.8 = f32[1,128,4096]{2,1,0:T(8,128)} copy(f32[1,128,4096]{2,1,0:T(8,128)} %bitcast.3) | data formatting | bytes 4194304
  37.8 0.0 copy-done
  37.8 0.6 %copy.9 = f32[16,256]{1,0:T(8,128)} copy(f32[16,256]{1,0:T(8,128)S(1)} %copy-done) | data formatting | bytes 32768
Async XLA Ops:
  34.7 3.1 %copy-start = (f32[16,256]{1,0:T(8,128)S(1)}, f32[16,256]{1,0:T(8,128)}, u32[]{:S(2)}) copy-start(f32[16,256]{1,0:T(8,128)} %get-tuple-element.9) | copy-start | bytes 49156
